TPU v7x, 32 devices: a whole 2x2x4 slice. The times are simulated.
32 devices in a mesh: tm: 4 (over y, x), slab: 8 (over z, core).
Axes of the slice: x: 2, y: 2, z: 4, core: 2. Of those that a mesh axis runs over, the one named last changes fastest.
Arguments:
- eigvecs: float32 [4, 3, 3456, 2, 128], P('tm', None, 'slab'), may hold values from -6 to 6
- perambulator: float32 [512, 8, 2, 512], P('slab', 'tm'), may hold values from -0.015625 to 0.015625
- time_pairs: int32 [8, 2], P('tm'), may hold values from 0 to 3
- momenta: int32 [4, 3], replicated, may hold values from -2 to 2, as said below
Outputs:
- dressed: float32 [512, 8, 4, 2, 512], P('slab', 'tm')
Inputs may be any that keep to these rules, and one draw needn't show every extreme that they name: `momenta`: every component of each momentum is nonzero.
All inputs are finite; a program needn't handle non-finite values.
Results may differ from a plain program's by a relative error of at most 0.0001.
Values sent between devices are 32-bit elements; how exact they have to be, the bound alone decides.
A program may use at most 64 MiB of HBM per device.

v0:
```python
import functools
import math

import jax
import jax.numpy as jnp
from jax import lax
from jax.experimental import pallas as pl
from jax.experimental.pallas import tpu as pltpu
from jax.sharding import PartitionSpec as P

LS = 48
SLABS = 8
TIMES = 4
BF16 = jnp.bfloat16
F32 = jnp.float32
NN = (((1,), (0,)), ((), ()))
NT = (((1,), (1,)), ((), ()))


def split(value):
    high = value.astype(BF16)
    return high, (value - high.astype(F32)).astype(BF16)


def dot3(left, right, dims):
    def one(x, y):
        return lax.dot_general(x, y, dims, preferred_element_type=F32)

    return one(left[0], right[0]) + (one(left[0], right[1]) + one(left[1], right[0]))


def floor_div(value, by):
    return jnp.floor((value + 0.5) * (1.0 / by))


def gather_kernel(
    scale, mom_ref, eig_ref, per_ref, e_ref, d_ref,
    lh, ll, rh, rl, phase, part, r1, r2, h2, r3, psend, precv,
    send_sem, recv_sem, psend_sem, precv_sem,
):
    slab = lax.axis_index("slab")
    time = lax.axis_index("tm")
    core = slab % 2
    sub = (slab // 2) % 2
    sibling = slab + 1 - 2 * core
    near = slab + 2 - 4 * sub
    far = (slab + 4) % SLABS
    tm_peers = (time + 1 - 2 * (time % 2), (time + 2) % TIMES, TIMES - 1 - time)
    slab_peers = (sibling, near, far)

    barrier = pltpu.get_barrier_semaphore()
    for peer in slab_peers:
        pl.semaphore_signal(barrier, inc=1, device_id={"slab": peer}, device_id_type=pl.DeviceIdType.MESH)
    for peer in tm_peers:
        pl.semaphore_signal(barrier, inc=1, device_id={"tm": peer}, device_id_type=pl.DeviceIdType.MESH)

    pairs = psend.shape[0]
    cols = psend.shape[2]
    for k in range(pairs):
        for p in range(2):
            spins = [
                per_ref[pl.ds(k * 8 + t * 2 + p, cols, stride=8 * pairs), :] for t in range(4)
            ]
            psend[k, p, :, 0:128] = spins[0] + spins[2]
            psend[k, p, :, 128:256] = spins[1] + spins[3]

    pl.semaphore_wait(barrier, len(slab_peers) + len(tm_peers))

    def remote(src, dst, ssem, rsem, axis, peer):
        return pltpu.make_async_remote_copy(
            src_ref=src, dst_ref=dst, send_sem=ssem, recv_sem=rsem,
            device_id={axis: peer}, device_id_type=pl.DeviceIdType.MESH,
        )

    p_far = remote(psend, precv, psend_sem.at[0], precv_sem.at[0], "slab", far)
    p_far.start()
    p_core = remote(d_ref.at[core], d_ref.at[core], psend_sem.at[1], precv_sem.at[1], "slab", sibling)

    moms = mom_ref.shape[0]
    sites = phase.shape[0]
    site = (lax.broadcasted_iota(jnp.int32, (sites, 128), 0) + slab * sites).astype(F32)
    lane = lax.broadcasted_iota(jnp.int32, (sites, 128), 1)
    row = floor_div(site, LS)
    plane = floor_div(row, LS)
    coords = (site - LS * row, row - LS * plane, plane)
    turns = jnp.zeros((sites, 128), F32)
    for m in range(moms):
        mine = mom_ref[m, 0].astype(F32) * coords[0]
        mine = mine + mom_ref[m, 1].astype(F32) * coords[1]
        mine = mine + mom_ref[m, 2].astype(F32) * coords[2]
        turns = jnp.where(lane % moms == m, mine, turns)
    turns = turns - LS * floor_div(turns, LS)
    turns = jnp.where(lane >= moms, turns - LS / 4, turns)
    phase[...] = jnp.cos(turns * (2.0 * math.pi / LS))

    colours = eig_ref.shape[0] // (2 * sites)
    for c in range(colours):
        real = eig_ref[pl.ds(2 * sites * c, sites, stride=2), :]
        imag = eig_ref[pl.ds(2 * sites * c + 1, sites, stride=2), :]
        high, low = split(jnp.concatenate([real, imag], axis=1))
        lh[c * sites:(c + 1) * sites, :] = high
        ll[c * sites:(c + 1) * sites, :] = low

    def compute(m):
        cosine = phase[:, m:m + 1]
        sine = phase[:, moms + m:moms + m + 1]
        for c in range(colours):
            real = eig_ref[pl.ds(2 * sites * c, sites, stride=2), :]
            imag = eig_ref[pl.ds(2 * sites * c + 1, sites, stride=2), :]
            turned = jnp.concatenate(
                [cosine * real - sine * imag, sine * real + cosine * imag], axis=1
            )
            high, low = split(turned)
            rh[c * sites:(c + 1) * sites, :] = high
            rl[c * sites:(c + 1) * sites, :] = low
        tn = (((0,), (0,)), ((), ()))
        got = dot3((lh[...], ll[...]), (rh[...], rl[...]), tn)
        both = (
            got[:128, :128] + got[128:, 128:],
            got[:128, 128:] - got[128:, :128],
        )
        for half in range(2):
            for u in range(2):
                for p in range(2):
                    start = half * 64 + u * 32
                    part[m, half, u, p] = both[p][start:start + 32]

    steps = {}

    def step1(m):
        steps[m, 1] = remote(
            part.at[m, 1 - core], r1.at[m], send_sem.at[m, 0], recv_sem.at[m, 0], "slab", sibling
        )
        steps[m, 1].start()

    def step2(m):
        steps[m, 1].wait_recv()
        part[m, core] = part[m, core] + r1[m]
        steps[m, 2] = remote(
            part.at[m, core, 1 - sub], r2.at[m], send_sem.at[m, 1], recv_sem.at[m, 1], "slab", near
        )
        steps[m, 2].start()

    def step3(m):
        steps[m, 2].wait_recv()
        h2[m] = part[m, core, sub] + r2[m]
        steps[m, 3] = remote(h2.at[m], r3.at[m], send_sem.at[m, 2], recv_sem.at[m, 2], "slab", far)
        steps[m, 3].start()

    def step4(m):
        steps[m, 3].wait_recv()
        e_ref[m, core, time, sub] = (h2[m] + r3[m]) * scale
        done = e_ref.at[m, core, time, sub]
        steps[m, 4] = remote(done, done, send_sem.at[m, 3], recv_sem.at[m, 3], "slab", near)
        steps[m, 4].start()

    def step5(m):
        steps[m, 4].wait_recv()
        done = e_ref.at[m, core, time]
        for n, peer in enumerate(tm_peers):
            steps[m, 5, n] = remote(
                done, done, send_sem.at[m, 4 + n], recv_sem.at[m, 4 + n], "tm", peer
            )
            steps[m, 5, n].start()

    def step6(m):
        for n in range(len(tm_peers)):
            steps[m, 5, n].wait_recv()
        done = e_ref.at[m, core]
        steps[m, 6] = remote(done, done, send_sem.at[m, 7], recv_sem.at[m, 7], "slab", sibling)
        steps[m, 6].start()

    def step7(m):
        steps[m, 6].wait_recv()

    stages = (step1, step2, step3, step4, step5, step6, step7)
    for tick in range(moms + len(stages) - 1):
        if tick < moms:
            compute(tick)
        if tick == moms:
            p_far.wait_recv()
            d_ref[core] = psend[...] - precv[...]
            p_core.start()
        for m in range(moms):
            if 0 <= tick - m < len(stages):
                stages[tick - m](m)

    p_core.wait_recv()
    p_far.wait_send()
    p_core.wait_send()
    for copy in steps.values():
        copy.wait_send()


def dress_kernel(pairs_ref, e_ref, d_ref, out_ref):
    core = lax.axis_index("slab") % 2
    moms = e_ref.shape[0]
    pairs = d_ref.shape[1]
    block = d_ref.shape[3]
    for k in range(pairs):
        t1 = pairs_ref[k, 0]
        t2 = pairs_ref[k, 1]
        source = jnp.concatenate(
            [
                jnp.concatenate(
                    [e_ref[m, core, t1, :, 0].reshape(64, 128), e_ref[m, core, t1, :, 1].reshape(64, 128)],
                    axis=1,
                )
                for m in range(moms)
            ],
            axis=0,
        )
        peram_re = d_ref[:, k, 0].reshape(2 * block, 256)
        peram_im = d_ref[:, k, 1].reshape(2 * block, 256)
        (rh, rl), (ih, il) = split(peram_re), split(peram_im)

        def wide(re, im):
            return jnp.concatenate(
                [jnp.concatenate([re, im], axis=1), jnp.concatenate([im, -re], axis=1)], axis=0
            )

        fold = dot3(split(source), (wide(rh, ih), wide(rl, il)), NN)
        for m in range(moms):
            mine = fold[64 * m:64 * (m + 1)]
            left = jnp.concatenate(
                [
                    jnp.concatenate([mine[:, 0:128], mine[:, 256:384]], axis=1),
                    jnp.concatenate([mine[:, 128:256], mine[:, 384:512]], axis=1),
                ],
                axis=0,
            )
            sink_re = jnp.concatenate(
                [e_ref[m, h, t2, :, 0].reshape(64, 128) for h in range(2)], axis=0
            )
            sink_im = jnp.concatenate(
                [e_ref[m, h, t2, :, 1].reshape(64, 128) for h in range(2)], axis=0
            )
            (sh, sl), (th, tl) = split(sink_re), split(sink_im)

            def tall(re, im):
                return jnp.concatenate(
                    [jnp.concatenate([re, -im], axis=1), jnp.concatenate([im, re], axis=1)], axis=0
                )

            got = dot3(split(left), (tall(sh, th), tall(sl, tl)), NT)
            for t in range(4):
                for p in range(2):
                    out_ref[pl.ds(((k * moms + m) * 4 + t) * 2 + p, 64, stride=8 * moms * pairs), :] = got[
                        64 * (t % 2):64 * (t % 2 + 1), 128 * p:128 * (p + 1)
                    ]


def kernel_shards(eigvecs, perambulator, time_pairs, momenta):
    _, colours, sites, _, vecs = eigvecs.shape
    cols, pairs, _, order = perambulator.shape
    moms = momenta.shape[0]
    scale = 1.0 / math.sqrt(2.0 * colours * sites * SLABS)
    eig_rows = eigvecs.reshape(colours * sites * 2, vecs)
    per_rows = (
        perambulator.reshape(cols, pairs, 2, 4, vecs)
        .transpose(0, 1, 3, 2, 4)
        .reshape(cols * pairs * 8, vecs)
    )
    vmem = pl.BlockSpec(memory_space=pltpu.VMEM)
    smem = pl.BlockSpec(memory_space=pltpu.SMEM)
    depth = colours * sites
    elems, dress = pl.pallas_call(
        functools.partial(gather_kernel, scale),
        out_shape=(
            jax.ShapeDtypeStruct((moms, 2, TIMES, 2, 2, 32, vecs), F32),
            jax.ShapeDtypeStruct((2, pairs, 2, cols, 2 * vecs), F32),
        ),
        in_specs=[smem, vmem, vmem],
        out_specs=(vmem, vmem),
        scratch_shapes=[
            pltpu.VMEM((depth, 2 * vecs), BF16),
            pltpu.VMEM((depth, 2 * vecs), BF16),
            pltpu.VMEM((depth, 2 * vecs), BF16),
            pltpu.VMEM((depth, 2 * vecs), BF16),
            pltpu.VMEM((sites, 128), F32),
            pltpu.VMEM((moms, 2, 2, 2, 32, vecs), F32),
            pltpu.VMEM((moms, 2, 2, 32, vecs), F32),
            pltpu.VMEM((moms, 2, 32, vecs), F32),
            pltpu.VMEM((moms, 2, 32, vecs), F32),
            pltpu.VMEM((moms, 2, 32, vecs), F32),
            pltpu.VMEM((pairs, 2, cols, 2 * vecs), F32),
            pltpu.VMEM((pairs, 2, cols, 2 * vecs), F32),
            pltpu.SemaphoreType.DMA((moms, 8)),
            pltpu.SemaphoreType.DMA((moms, 8)),
            pltpu.SemaphoreType.DMA((2,)),
            pltpu.SemaphoreType.DMA((2,)),
        ],
        compiler_params=pltpu.CompilerParams(
            collective_id=0, has_side_effects=True, vmem_limit_bytes=40 * 2**20
        ),
        name="elementals",
    )(momenta, eig_rows, per_rows)
    rows = pl.pallas_call(
        dress_kernel,
        out_shape=jax.ShapeDtypeStruct((cols * pairs * moms * 8, vecs), F32),
        in_specs=[smem, vmem, vmem],
        out_specs=vmem,
        compiler_params=pltpu.CompilerParams(vmem_limit_bytes=40 * 2**20),
        name="dressing",
    )(time_pairs, elems, dress)
    return (
        rows.reshape(cols, pairs, moms, 4, 2, vecs)
        .transpose(0, 1, 2, 4, 3, 5)
        .reshape(cols, pairs, moms, 2, order)
    )


PRECISE = lax.Precision.HIGHEST
SPIN_MIX = ((1.0, 0.0, 1.0, 0.0), (0.0, 1.0, 0.0, 1.0), (1.0, 0.0, 1.0, 0.0), (0.0, 1.0, 0.0, 1.0))
CHIRAL = (1.0, 1.0, -1.0, -1.0)


def spin_tables():
    spin_mix = jnp.array(SPIN_MIX, jnp.float32)
    chiral = jnp.array(CHIRAL, jnp.float32)
    spin_dressed = chiral[:, None] * spin_mix * chiral[None, :]
    return (spin_mix, spin_dressed)


def phase_tables(momenta, site_ids):
    coords = jnp.stack([site_ids % LS, site_ids // LS % LS, site_ids // (LS * LS)])
    phase_turns = jnp.mod(jnp.sum(momenta[:, :, None] * coords[None, :, :], axis=1), LS)
    phase_angle = phase_turns.astype(jnp.float32) * (2.0 * math.pi / LS)
    return (jnp.cos(phase_angle), jnp.sin(phase_angle))


def elemental_terms(vectors, cosine_tab, sine_tab):
    local_times = vectors.shape[0]
    vec_count = vectors.shape[4]
    real_part = vectors[:, :, :, 0, :]
    imag_part = vectors[:, :, :, 1, :]
    left_rows = vectors.reshape(local_times, -1, vec_count)
    per_moment = []
    for mom_index in range(cosine_tab.shape[0]):
        cos_here = cosine_tab[mom_index][None, None, :, None]
        sin_here = sine_tab[mom_index][None, None, :, None]
        turned_re = cos_here * real_part - sin_here * imag_part
        turned_im = sin_here * real_part + cos_here * imag_part
        first_half = jnp.stack([turned_re, turned_im], axis=3).reshape(local_times, -1, vec_count)
        second_half = jnp.stack([turned_im, -turned_re], axis=3).reshape(local_times, -1, vec_count)
        right_cols = jnp.concatenate([first_half, second_half], axis=2)
        product = jnp.einsum("tki,tkj->tij", left_rows, right_cols, precision=PRECISE)
        per_moment.append(
            product.reshape(local_times, vec_count, 2, vec_count).transpose(0, 2, 1, 3)
        )
    return jnp.stack(per_moment, axis=1)


def shards(eigvecs, perambulator, time_pairs, momenta):
    colour_count = eigvecs.shape[1]
    site_count = eigvecs.shape[2]
    vec_count = eigvecs.shape[4]
    slab_count = lax.axis_size("slab")
    site_ids = lax.axis_index("slab") * site_count + jnp.arange(site_count, dtype=jnp.int32)
    cosine_tab, sine_tab = phase_tables(momenta, site_ids)
    partial_sums = elemental_terms(eigvecs, cosine_tab, sine_tab)
    summed = lax.psum(partial_sums, "slab")
    all_times = lax.all_gather(summed, "tm", axis=0, tiled=True)
    all_times = all_times * (1.0 / math.sqrt(2.0 * colour_count * site_count * slab_count))
    sink_elem = jnp.take(all_times, time_pairs[:, 1], axis=0)
    source_elem = jnp.take(all_times, time_pairs[:, 0], axis=0)
    sink_re = sink_elem[:, :, 0]
    sink_im = sink_elem[:, :, 1]
    spin_mix, spin_dressed = spin_tables()
    panel_cols = perambulator.shape[0]
    pair_count = perambulator.shape[1]
    spin_order = perambulator.shape[3]
    spin_count = spin_order // vec_count
    mom_count = momenta.shape[0]
    panel_start = lax.axis_index("slab") * panel_cols
    panel_spin = panel_start // vec_count
    panel_vec = panel_start % vec_count
    chiral_col = lax.dynamic_index_in_dim(spin_dressed, panel_spin, 1, keepdims=False)
    source_block = lax.dynamic_slice_in_dim(source_elem, panel_vec, panel_cols, 3)
    dress_re = jnp.einsum("s,kmbi->kmsib", chiral_col, source_block[:, :, 0]).reshape(
        pair_count, mom_count, spin_order, panel_cols
    )
    dress_im = -jnp.einsum("s,kmbi->kmsib", chiral_col, source_block[:, :, 1]).reshape(
        pair_count, mom_count, spin_order, panel_cols
    )
    peram_piece = lax.all_gather(perambulator, "slab", axis=0, tiled=True)
    piece_re = peram_piece[:, :, 0]
    piece_im = peram_piece[:, :, 1]
    fold_re = jnp.einsum("ckr,kmcb->bkmr", piece_re, dress_re, precision=PRECISE) - jnp.einsum(
        "ckr,kmcb->bkmr", piece_im, dress_im, precision=PRECISE
    )
    fold_im = jnp.einsum("ckr,kmcb->bkmr", piece_re, dress_im, precision=PRECISE) + jnp.einsum(
        "ckr,kmcb->bkmr", piece_im, dress_re, precision=PRECISE
    )
    fold_re, fold_im = (fold_re, fold_im)
    fold_re = fold_re.reshape(panel_cols, pair_count, mom_count, spin_count, vec_count)
    fold_im = fold_im.reshape(panel_cols, pair_count, mom_count, spin_count, vec_count)
    mixed_re = jnp.einsum("bkmsj,kmij->bkmsi", fold_re, sink_re, precision=PRECISE) - jnp.einsum(
        "bkmsj,kmij->bkmsi", fold_im, sink_im, precision=PRECISE
    )
    mixed_im = jnp.einsum("bkmsj,kmij->bkmsi", fold_re, sink_im, precision=PRECISE) + jnp.einsum(
        "bkmsj,kmij->bkmsi", fold_im, sink_re, precision=PRECISE
    )
    final_re = jnp.einsum("ts,bkmsi->bkmti", spin_mix, mixed_re, precision=PRECISE).reshape(
        panel_cols, pair_count, mom_count, spin_order
    )
    final_im = jnp.einsum("ts,bkmsi->bkmti", spin_mix, mixed_im, precision=PRECISE).reshape(
        panel_cols, pair_count, mom_count, spin_order
    )
    dressed = jnp.stack([final_re, final_im], axis=3)
    return dressed


def solution(mesh):
    known = mesh.shape["tm"] == TIMES and mesh.shape["slab"] == SLABS
    return jax.shard_map(
        kernel_shards if known else shards,
        mesh=mesh,
        in_specs=(
            P("tm", None, "slab", None, None),
            P("slab", "tm", None, None),
            P("tm", None),
            P(),
        ),
        out_specs=P("slab", "tm", None, None, None),
        check_vma=False,
    )
```

profile of v0, /device:TPU:1, one launch (start us, length us, event | category | flops | bytes accessed | tf_op | source)
XLA Modules:
  0.0 53.2 jit_solution(13802063918147189727)
XLA Ops:
  0.0 0.0 copy-start
  0.0 1.3 %copy-done = f32[1,3,432,2,128]{4,3,2,1,0:T(2,128)S(1)} copy-done((f32[1,3,432,2,128]{4,3,2,1,0:T(2,128)S(1)}, f32[1,3,432,2,128]{4,3,2,1,0:T(2,128)}, u32[]{:S(2)}) %copy-start) | copy-done | bytes 1327128
  1.3 0.0 copy-start.1
  1.3 1.0 %copy-done.1 = f32[64,2,2,512]{3,2,1,0:T(2,128)S(1)} copy-done((f32[64,2,2,512]{3,2,1,0:T(2,128)S(1)}, f32[64,2,2,512]{3,2,1,0:T(2,128)}, u32[]{:S(2)}) %copy-start.1) | copy-done | bytes 524312
  2.4 0.0 copy-start.2
  2.4 0.7 %copy-done.2 = s32[4,3]{1,0:T(4,128)S(1)} copy-done((s32[4,3]{1,0:T(4,128)S(1)}, s32[4,3]{1,0:T(4,128)}, u32[]{:S(2)}) %copy-start.2) | copy-done | bytes 72
  3.0 45.1 %elementals.1 = (f32[4,2,4,2,2,32,128]{6,5,4,3,2,1,0:T(8,128)S(1)}, f32[2,2,2,64,256]{4,3,2,1,0:T(8,128)S(1)}) custom-call(s32[4,3]{1,0:T(4,128)S(1)} %copy-done.2, f32[2592,128]{1,0:T(8,128)S(1)} %bitcast.11, f32[1024,128]{1,0:T(8,128)S(1)} %bitcast.12), custom_call_target="tpu_custom_call" | custom-call | tf_op jit(solution)/shard_map/elementals/pallas_call | solution.py:267
  48.1 0.0 copy-start.3
  48.1 0.7 %copy-done.3 = s32[2,2]{1,0:T(2,128)S(1)} copy-done((s32[2,2]{1,0:T(2,128)S(1)}, s32[2,2]{1,0:T(2,128)}, u32[]{:S(2)}) %copy-start.3) | copy-done | bytes 40
  48.8 4.4 %dressing.1 = f32[4096,128]{1,0:T(8,128)} custom-call(s32[2,2]{1,0:T(2,128)S(1)} %copy-done.3, f32[4,2,4,2,2,32,128]{6,5,4,3,2,1,0:T(8,128)S(1)} %get-tuple-element.7.e_ref, f32[2,2,2,64,256]{4,3,2,1,0:T(8,128)S(1)} %get-tuple-element.8.d_ref), custom_call_target="tpu_custom_call" | custom-call | tf_op jit(solution)/shard_map/dressing/pallas_call | solution.py:298
Async XLA Ops:
  0.0 1.3 %copy-start = (f32[1,3,432,2,128]{4,3,2,1,0:T(2,128)S(1)}, f32[1,3,432,2,128]{4,3,2,1,0:T(2,128)}, u32[]{:S(2)}) copy-start(f32[1,3,432,2,128]{4,3,2,1,0:T(2,128)} %param.4) | copy-start | bytes 3981316
  1.3 1.0 %copy-start.1 = (f32[64,2,2,512]{3,2,1,0:T(2,128)S(1)}, f32[64,2,2,512]{3,2,1,0:T(2,128)}, u32[]{:S(2)}) copy-start(f32[64,2,2,512]{3,2,1,0:T(2,128)} %param.5) | copy-start | bytes 1572868
  2.4 0.7 %copy-start.2 = (s32[4,3]{1,0:T(4,128)S(1)}, s32[4,3]{1,0:T(4,128)}, u32[]{:S(2)}) copy-start(s32[4,3]{1,0:T(4,128)} %mom_ref.1) | copy-start | bytes 148
  48.1 0.7 %copy-start.3 = (s32[2,2]{1,0:T(2,128)S(1)}, s32[2,2]{1,0:T(2,128)}, u32[]{:S(2)}) copy-start(s32[2,2]{1,0:T(2,128)} %pairs_ref.1) | copy-start | bytes 52
where the time goes:
time: 53.5 us; the launch traced here: 53.2 us
  Pallas kernels  49.5 us (93%)
  local copies, waits for them, and re-layouts  3.72 us (7%)
    pallas_call x1, Pallas kernels, kernel_shards(): pl.pallas_call(functools.partial(gather_kernel, scale), out_shape=(jax.Sh...  45.1 us
    pallas_call x1, Pallas kernels, kernel_shards(): pl.pallas_call(dress_kernel, out_shape=jax.ShapeDtypeStruct((cols * pairs...  4.41 us
    unnamed x8, local copies, waits for them, and re-layouts  3.72 us

commit v1 on v0

--- a/solution.py
+++ b/solution.py
@@ -33,9 +33,9 @@
     return jnp.floor((value + 0.5) * (1.0 / by))
 
 
-def gather_kernel(
-    scale, mom_ref, eig_ref, per_ref, e_ref, d_ref,
-    lh, ll, rh, rl, phase, part, r1, r2, h2, r3, psend, precv,
+def correlator_kernel(
+    scale, mom_hbm, eig_hbm, per_hbm, pairs_hbm, out_hbm,
+    e_refs, d_ref, out_ref, out_sem, pairs_ref, mom_ref, eig_ref, per_ref, load_sem, left, rh, rl, phase, part, r1, r2, h2, r3, psend, precv,
     send_sem, recv_sem, psend_sem, precv_sem,
 ):
     slab = lax.axis_index("slab")
@@ -48,12 +48,22 @@
     tm_peers = (time + 1 - 2 * (time % 2), (time + 2) % TIMES, TIMES - 1 - time)
     slab_peers = (sibling, near, far)
 
+    loads = [
+        pltpu.make_async_copy(src, dst, load_sem.at[n])
+        for n, (src, dst) in enumerate(
+            ((per_hbm, per_ref), (mom_hbm, mom_ref), (eig_hbm, eig_ref), (pairs_hbm, pairs_ref))
+        )
+    ]
+    for load in loads:
+        load.start()
+
     barrier = pltpu.get_barrier_semaphore()
     for peer in slab_peers:
         pl.semaphore_signal(barrier, inc=1, device_id={"slab": peer}, device_id_type=pl.DeviceIdType.MESH)
     for peer in tm_peers:
         pl.semaphore_signal(barrier, inc=1, device_id={"tm": peer}, device_id_type=pl.DeviceIdType.MESH)
 
+    loads[0].wait()
     pairs = psend.shape[0]
     cols = psend.shape[2]
     for k in range(pairs):
@@ -72,9 +82,22 @@
             device_id={axis: peer}, device_id_type=pl.DeviceIdType.MESH,
         )
 
-    p_far = remote(psend, precv, psend_sem.at[0], precv_sem.at[0], "slab", far)
-    p_far.start()
-    p_core = remote(d_ref.at[core], d_ref.at[core], psend_sem.at[1], precv_sem.at[1], "slab", sibling)
+    p_far = [
+        remote(psend.at[k], precv.at[k], psend_sem.at[0, k], precv_sem.at[0, k], "slab", far)
+        for k in range(pairs)
+    ]
+    p_core = [
+        remote(d_ref.at[core, k], d_ref.at[core, k], psend_sem.at[1, k], precv_sem.at[1, k], "slab", sibling)
+        for k in range(pairs)
+    ]
+
+    def difference(k):
+        p_far[k].wait_recv()
+        d_ref[core, k] = psend[k] - precv[k]
+        p_core[k].start()
+
+    p_far[0].start()
+    loads[1].wait()
 
     moms = mom_ref.shape[0]
     sites = phase.shape[0]
@@ -93,13 +116,17 @@
     turns = jnp.where(lane >= moms, turns - LS / 4, turns)
     phase[...] = jnp.cos(turns * (2.0 * math.pi / LS))
 
+    loads[2].wait()
+    rows = []
     colours = eig_ref.shape[0] // (2 * sites)
     for c in range(colours):
         real = eig_ref[pl.ds(2 * sites * c, sites, stride=2), :]
         imag = eig_ref[pl.ds(2 * sites * c + 1, sites, stride=2), :]
-        high, low = split(jnp.concatenate([real, imag], axis=1))
-        lh[c * sites:(c + 1) * sites, :] = high
-        ll[c * sites:(c + 1) * sites, :] = low
+        rows.append(jnp.concatenate([real, imag], axis=1))
+    high, low = split(jnp.concatenate(rows, axis=0).T)
+    wide = rows[0].shape[1]
+    left[:wide] = high
+    left[wide:] = low
 
     def compute(m):
         cosine = phase[:, m:m + 1]
@@ -113,8 +140,9 @@
             high, low = split(turned)
             rh[c * sites:(c + 1) * sites, :] = high
             rl[c * sites:(c + 1) * sites, :] = low
-        tn = (((0,), (0,)), ((), ()))
-        got = dot3((lh[...], ll[...]), (rh[...], rl[...]), tn)
+        coarse = lax.dot_general(left[...], rh[...], NN, preferred_element_type=F32)
+        fine = lax.dot_general(left[:wide], rl[...], NN, preferred_element_type=F32)
+        got = coarse[:wide] + (coarse[wide:] + fine)
         both = (
             got[:128, :128] + got[128:, 128:],
             got[:128, 128:] - got[128:, :128],
@@ -149,14 +177,14 @@
 
     def step4(m):
         steps[m, 3].wait_recv()
-        e_ref[m, core, time, sub] = (h2[m] + r3[m]) * scale
-        done = e_ref.at[m, core, time, sub]
+        e_refs[m][core, time, sub] = (h2[m] + r3[m]) * scale
+        done = e_refs[m].at[core, time, sub]
         steps[m, 4] = remote(done, done, send_sem.at[m, 3], recv_sem.at[m, 3], "slab", near)
         steps[m, 4].start()
 
     def step5(m):
         steps[m, 4].wait_recv()
-        done = e_ref.at[m, core, time]
+        done = e_refs[m].at[core, time]
         for n, peer in enumerate(tm_peers):
             steps[m, 5, n] = remote(
                 done, done, send_sem.at[m, 4 + n], recv_sem.at[m, 4 + n], "tm", peer
@@ -166,88 +194,91 @@
     def step6(m):
         for n in range(len(tm_peers)):
             steps[m, 5, n].wait_recv()
-        done = e_ref.at[m, core]
+        done = e_refs[m].at[core]
         steps[m, 6] = remote(done, done, send_sem.at[m, 7], recv_sem.at[m, 7], "slab", sibling)
         steps[m, 6].start()
 
     def step7(m):
         steps[m, 6].wait_recv()
-
+        if m == 0:
+            for copy in p_core:
+                copy.wait_recv()
+            loads[3].wait()
+        for k in range(pairs):
+            dress(m, k)
+        rows = cols * pairs * 8
+        stores[m] = pltpu.make_async_copy(
+            out_ref.at[pl.ds(m * rows, rows)].reshape(cols, pairs, 8, 128),
+            out_hbm.at[:, :, m],
+            out_sem.at[m],
+        )
+        stores[m].start()
+
+    def dress(m, k):
+        e_ref = e_refs[m]
+        t1 = pairs_ref[k, 0]
+        t2 = pairs_ref[k, 1]
+
+        def block(half, t, p):
+            return e_ref[half, t, :, p].reshape(64, 128)
+
+        source = split(jnp.concatenate([block(core, t1, 0), block(core, t1, 1)], axis=1))
+        re_high, re_low = split(d_ref[:, k, 0].reshape(2 * cols, 256))
+        im_high, im_low = split(d_ref[:, k, 1].reshape(2 * cols, 256))
+
+        def wide_of(re, im):
+            return jnp.concatenate(
+                [jnp.concatenate([re, im], axis=1), jnp.concatenate([im, -re], axis=1)], axis=0
+            )
+
+        fold = dot3(source, (wide_of(re_high, im_high), wide_of(re_low, im_low)), NN)
+        spun = jnp.concatenate(
+            [
+                jnp.concatenate([fold[:, 0:128], fold[:, 256:384]], axis=1),
+                jnp.concatenate([fold[:, 128:256], fold[:, 384:512]], axis=1),
+            ],
+            axis=0,
+        )
+        sink = [
+            split(jnp.concatenate([block(0, t2, p), block(1, t2, p)], axis=0)) for p in range(2)
+        ]
+
+        def tall_of(re, im):
+            return jnp.concatenate(
+                [jnp.concatenate([re, -im], axis=1), jnp.concatenate([im, re], axis=1)], axis=0
+            )
+
+        right = tuple(tall_of(sink[0][n], sink[1][n]) for n in range(2))
+        got = dot3(split(spun), right, NT)
+        for t in range(4):
+            for p in range(2):
+                start = m * cols * pairs * 8 + k * 8 + t * 2 + p
+                out_ref[pl.ds(start, cols, stride=8 * pairs), :] = got[
+                    64 * (t % 2):64 * (t % 2 + 1), 128 * p:128 * (p + 1)
+                ]
+
+    stores = {}
     stages = (step1, step2, step3, step4, step5, step6, step7)
     for tick in range(moms + len(stages) - 1):
         if tick < moms:
             compute(tick)
-        if tick == moms:
-            p_far.wait_recv()
-            d_ref[core] = psend[...] - precv[...]
-            p_core.start()
+        if tick == moms + 2:
+            for k in range(1, pairs):
+                difference(k)
         for m in range(moms):
             if 0 <= tick - m < len(stages):
                 stages[tick - m](m)
-
-    p_core.wait_recv()
-    p_far.wait_send()
-    p_core.wait_send()
+        if tick == moms:
+            for k in range(1, pairs):
+                p_far[k].start()
+            difference(0)
+
+    for copy in p_far + p_core:
+        copy.wait_send()
     for copy in steps.values():
         copy.wait_send()
-
-
-def dress_kernel(pairs_ref, e_ref, d_ref, out_ref):
-    core = lax.axis_index("slab") % 2
-    moms = e_ref.shape[0]
-    pairs = d_ref.shape[1]
-    block = d_ref.shape[3]
-    for k in range(pairs):
-        t1 = pairs_ref[k, 0]
-        t2 = pairs_ref[k, 1]
-        source = jnp.concatenate(
-            [
-                jnp.concatenate(
-                    [e_ref[m, core, t1, :, 0].reshape(64, 128), e_ref[m, core, t1, :, 1].reshape(64, 128)],
-                    axis=1,
-                )
-                for m in range(moms)
-            ],
-            axis=0,
-        )
-        peram_re = d_ref[:, k, 0].reshape(2 * block, 256)
-        peram_im = d_ref[:, k, 1].reshape(2 * block, 256)
-        (rh, rl), (ih, il) = split(peram_re), split(peram_im)
-
-        def wide(re, im):
-            return jnp.concatenate(
-                [jnp.concatenate([re, im], axis=1), jnp.concatenate([im, -re], axis=1)], axis=0
-            )
-
-        fold = dot3(split(source), (wide(rh, ih), wide(rl, il)), NN)
-        for m in range(moms):
-            mine = fold[64 * m:64 * (m + 1)]
-            left = jnp.concatenate(
-                [
-                    jnp.concatenate([mine[:, 0:128], mine[:, 256:384]], axis=1),
-                    jnp.concatenate([mine[:, 128:256], mine[:, 384:512]], axis=1),
-                ],
-                axis=0,
-            )
-            sink_re = jnp.concatenate(
-                [e_ref[m, h, t2, :, 0].reshape(64, 128) for h in range(2)], axis=0
-            )
-            sink_im = jnp.concatenate(
-                [e_ref[m, h, t2, :, 1].reshape(64, 128) for h in range(2)], axis=0
-            )
-            (sh, sl), (th, tl) = split(sink_re), split(sink_im)
-
-            def tall(re, im):
-                return jnp.concatenate(
-                    [jnp.concatenate([re, -im], axis=1), jnp.concatenate([im, re], axis=1)], axis=0
-                )
-
-            got = dot3(split(left), (tall(sh, th), tall(sl, tl)), NT)
-            for t in range(4):
-                for p in range(2):
-                    out_ref[pl.ds(((k * moms + m) * 4 + t) * 2 + p, 64, stride=8 * moms * pairs), :] = got[
-                        64 * (t % 2):64 * (t % 2 + 1), 128 * p:128 * (p + 1)
-                    ]
+    for store in stores.values():
+        store.wait()
 
 
 def kernel_shards(eigvecs, perambulator, time_pairs, momenta):
@@ -261,20 +292,24 @@
         .transpose(0, 1, 3, 2, 4)
         .reshape(cols * pairs * 8, vecs)
     )
-    vmem = pl.BlockSpec(memory_space=pltpu.VMEM)
-    smem = pl.BlockSpec(memory_space=pltpu.SMEM)
+    hbm = pl.BlockSpec(memory_space=pltpu.HBM)
     depth = colours * sites
-    elems, dress = pl.pallas_call(
-        functools.partial(gather_kernel, scale),
-        out_shape=(
-            jax.ShapeDtypeStruct((moms, 2, TIMES, 2, 2, 32, vecs), F32),
-            jax.ShapeDtypeStruct((2, pairs, 2, cols, 2 * vecs), F32),
-        ),
-        in_specs=[smem, vmem, vmem],
-        out_specs=(vmem, vmem),
+    rows = pl.pallas_call(
+        functools.partial(correlator_kernel, scale),
+        out_shape=jax.ShapeDtypeStruct((cols, pairs, moms, 8, vecs), F32),
+        in_specs=[hbm, hbm, hbm, hbm],
+        out_specs=hbm,
         scratch_shapes=[
-            pltpu.VMEM((depth, 2 * vecs), BF16),
-            pltpu.VMEM((depth, 2 * vecs), BF16),
+            [pltpu.VMEM((2, TIMES, 2, 2, 32, vecs), F32) for _ in range(moms)],
+            pltpu.VMEM((2, pairs, 2, cols, 2 * vecs), F32),
+            pltpu.VMEM((moms * cols * pairs * 8, vecs), F32),
+            pltpu.SemaphoreType.DMA((moms,)),
+            pltpu.SMEM(time_pairs.shape, jnp.int32),
+            pltpu.SMEM(momenta.shape, jnp.int32),
+            pltpu.VMEM(eig_rows.shape, F32),
+            pltpu.VMEM(per_rows.shape, F32),
+            pltpu.SemaphoreType.DMA((4,)),
+            pltpu.VMEM((4 * vecs, depth), BF16),
             pltpu.VMEM((depth, 2 * vecs), BF16),
             pltpu.VMEM((depth, 2 * vecs), BF16),
             pltpu.VMEM((sites, 128), F32),
@@ -287,22 +322,14 @@
             pltpu.VMEM((pairs, 2, cols, 2 * vecs), F32),
             pltpu.SemaphoreType.DMA((moms, 8)),
             pltpu.SemaphoreType.DMA((moms, 8)),
-            pltpu.SemaphoreType.DMA((2,)),
-            pltpu.SemaphoreType.DMA((2,)),
+            pltpu.SemaphoreType.DMA((2, pairs)),
+            pltpu.SemaphoreType.DMA((2, pairs)),
         ],
         compiler_params=pltpu.CompilerParams(
-            collective_id=0, has_side_effects=True, vmem_limit_bytes=40 * 2**20
+            collective_id=0, has_side_effects=True, vmem_limit_bytes=61 * 2**20
         ),
-        name="elementals",
-    )(momenta, eig_rows, per_rows)
-    rows = pl.pallas_call(
-        dress_kernel,
-        out_shape=jax.ShapeDtypeStruct((cols * pairs * moms * 8, vecs), F32),
-        in_specs=[smem, vmem, vmem],
-        out_specs=vmem,
-        compiler_params=pltpu.CompilerParams(vmem_limit_bytes=40 * 2**20),
-        name="dressing",
-    )(time_pairs, elems, dress)
+        name="correlators",
+    )(momenta, eig_rows, per_rows, time_pairs)
     return (
         rows.reshape(cols, pairs, moms, 4, 2, vecs)
         .transpose(0, 1, 2, 4, 3, 5)

time: 53.5 us -> 48.1 us (0.90)
  Pallas kernels: 49.5 us -> 43.5 us
  local copies, waits for them, and re-layouts: 3.72 us -> 4.41 us
    pallas_call x2 -> x1, Pallas kernels: 49.5 us -> 43.5 us  [kernel_shards(): pl.pallas_call(functools.partial(correlator_kernel, scale), out_shape=jax...]
    unnamed x8 -> x1, local copies, waits for them, and re-layouts: 3.72 us -> 4.41 us
where the time goes in v1:
time: 48.1 us; the launch traced here: 47.9 us
  Pallas kernels  43.5 us (90%)
  local copies, waits for them, and re-layouts  4.41 us (9%)
    pallas_call x1, Pallas kernels, kernel_shards(): pl.pallas_call(functools.partial(correlator_kernel, scale), out_shape=jax...  43.5 us
    unnamed x1, local copies, waits for them, and re-layouts  4.41 us

profile of v1, /device:TPU:1, one launch (start us, length us, event | category | flops | bytes accessed | tf_op | source)
XLA Modules:
  0.0 47.9 jit_solution(4808499418555703930)
XLA Ops:
  0.0 43.5 %correlators.1 = f32[64,2,4,8,128]{4,3,2,1,0:T(8,128)} custom-call(s32[4,3]{1,0:T(4,128)} %mom_hbm.1, f32[2592,128]{1,0:T(8,128)} %bitcast.12, f32[1024,128]{1,0:T(8,128)} %bitcast.13, s32[2,2]{1,0:T(2,128)} %pairs_hbm.1), custom_call_target="tpu_custom_call" | custom-call | tf_op jit(solution)/shard_map/correlators/pallas_call | solution.py:297
  43.5 4.4 %copy.8 = f32[64,2,4,2,512]{4,3,2,1,0:T(2,128)} copy(f32[64,2,4,2,512]{4,3,2,1,0:T(2,128)} %bitcast.11) | data formatting | bytes 4194304

commit v2 on v1

--- a/solution.py
+++ b/solution.py
@@ -11,6 +11,7 @@
 LS = 48
 SLABS = 8
 TIMES = 4
+PARTS = 4
 BF16 = jnp.bfloat16
 F32 = jnp.float32
 NN = (((1,), (0,)), ((), ()))
@@ -35,7 +36,7 @@
 
 def correlator_kernel(
     scale, mom_hbm, eig_hbm, per_hbm, pairs_hbm, out_hbm,
-    e_refs, d_ref, out_ref, out_sem, pairs_ref, mom_ref, eig_ref, per_ref, load_sem, left, rh, rl, phase, part, r1, r2, h2, r3, psend, precv,
+    e_refs, d_ref, out_ref, out_sem, pairs_ref, mom_ref, eig_ref, per_ref, load_sem, left, rh, rl, phase, part, r1, h2, r3, psend, precv,
     send_sem, recv_sem, psend_sem, precv_sem,
 ):
     slab = lax.axis_index("slab")
@@ -44,9 +45,10 @@
     sub = (slab // 2) % 2
     sibling = slab + 1 - 2 * core
     near = slab + 2 - 4 * sub
+    cross = near + 1 - 2 * core
     far = (slab + 4) % SLABS
     tm_peers = (time + 1 - 2 * (time % 2), (time + 2) % TIMES, TIMES - 1 - time)
-    slab_peers = (sibling, near, far)
+    slab_peers = (sibling, near, cross, far)
 
     loads = [
         pltpu.make_async_copy(src, dst, load_sem.at[n])
@@ -156,63 +158,52 @@
     steps = {}
 
     def step1(m):
-        steps[m, 1] = remote(
-            part.at[m, 1 - core], r1.at[m], send_sem.at[m, 0], recv_sem.at[m, 0], "slab", sibling
-        )
-        steps[m, 1].start()
+        for n, (half, u, peer) in enumerate(
+            ((1 - core, sub, sibling), (core, 1 - sub, near), (1 - core, 1 - sub, cross))
+        ):
+            steps[m, 1, n] = remote(
+                part.at[m, half, u], r1.at[m, n], send_sem.at[m, n], recv_sem.at[m, n], "slab", peer
+            )
+            steps[m, 1, n].start()
 
     def step2(m):
-        steps[m, 1].wait_recv()
-        part[m, core] = part[m, core] + r1[m]
-        steps[m, 2] = remote(
-            part.at[m, core, 1 - sub], r2.at[m], send_sem.at[m, 1], recv_sem.at[m, 1], "slab", near
-        )
+        for n in range(3):
+            steps[m, 1, n].wait_recv()
+        h2[m] = (part[m, core, sub] + r1[m, 0]) + (r1[m, 1] + r1[m, 2])
+        steps[m, 2] = remote(h2.at[m], r3.at[m], send_sem.at[m, 3], recv_sem.at[m, 3], "slab", far)
         steps[m, 2].start()
 
     def step3(m):
         steps[m, 2].wait_recv()
-        h2[m] = part[m, core, sub] + r2[m]
-        steps[m, 3] = remote(h2.at[m], r3.at[m], send_sem.at[m, 2], recv_sem.at[m, 2], "slab", far)
+        e_refs[m][core, time, sub] = (h2[m] + r3[m]) * scale
+        done = e_refs[m].at[core, time, sub]
+        steps[m, 3] = remote(done, done, send_sem.at[m, 4], recv_sem.at[m, 4], "slab", near)
         steps[m, 3].start()
 
     def step4(m):
         steps[m, 3].wait_recv()
-        e_refs[m][core, time, sub] = (h2[m] + r3[m]) * scale
-        done = e_refs[m].at[core, time, sub]
-        steps[m, 4] = remote(done, done, send_sem.at[m, 3], recv_sem.at[m, 3], "slab", near)
-        steps[m, 4].start()
-
-    def step5(m):
-        steps[m, 4].wait_recv()
         done = e_refs[m].at[core, time]
         for n, peer in enumerate(tm_peers):
-            steps[m, 5, n] = remote(
-                done, done, send_sem.at[m, 4 + n], recv_sem.at[m, 4 + n], "tm", peer
+            steps[m, 4, n] = remote(
+                done, done, send_sem.at[m, 5 + n], recv_sem.at[m, 5 + n], "tm", peer
             )
-            steps[m, 5, n].start()
+            steps[m, 4, n].start()
+
+    def step5(m):
+        for n in range(len(tm_peers)):
+            steps[m, 4, n].wait_recv()
+        done = e_refs[m].at[core]
+        steps[m, 5] = remote(done, done, send_sem.at[m, 8], recv_sem.at[m, 8], "slab", sibling)
+        steps[m, 5].start()
 
     def step6(m):
-        for n in range(len(tm_peers)):
-            steps[m, 5, n].wait_recv()
-        done = e_refs[m].at[core]
-        steps[m, 6] = remote(done, done, send_sem.at[m, 7], recv_sem.at[m, 7], "slab", sibling)
-        steps[m, 6].start()
-
-    def step7(m):
-        steps[m, 6].wait_recv()
+        steps[m, 5].wait_recv()
         if m == 0:
-            for copy in p_core:
-                copy.wait_recv()
+            p_core[0].wait_recv()
             loads[3].wait()
-        for k in range(pairs):
-            dress(m, k)
-        rows = cols * pairs * 8
-        stores[m] = pltpu.make_async_copy(
-            out_ref.at[pl.ds(m * rows, rows)].reshape(cols, pairs, 8, 128),
-            out_hbm.at[:, :, m],
-            out_sem.at[m],
-        )
-        stores[m].start()
+        dress(m, 0)
+
+    rows_each = cols * 8
 
     def dress(m, k):
         e_ref = e_refs[m]
@@ -252,26 +243,38 @@
         got = dot3(split(spun), right, NT)
         for t in range(4):
             for p in range(2):
-                start = m * cols * pairs * 8 + k * 8 + t * 2 + p
-                out_ref[pl.ds(start, cols, stride=8 * pairs), :] = got[
+                start = (m * pairs + k) * rows_each + t * 2 + p
+                out_ref[pl.ds(start, cols, stride=8), :] = got[
                     64 * (t % 2):64 * (t % 2 + 1), 128 * p:128 * (p + 1)
                 ]
+        stores[m, k] = pltpu.make_async_copy(
+            out_ref.at[pl.ds((m * pairs + k) * rows_each, rows_each)].reshape(cols, 8, 128),
+            out_hbm.at[:, k, m],
+            out_sem.at[m, k],
+        )
+        stores[m, k].start()
 
     stores = {}
-    stages = (step1, step2, step3, step4, step5, step6, step7)
-    for tick in range(moms + len(stages) - 1):
+    stages = (step1, step2, step3, step4, step5, step6)
+    ticks = moms + len(stages) - 1
+    for tick in range(ticks):
         if tick < moms:
             compute(tick)
-        if tick == moms + 2:
+        if tick == ticks - 1:
             for k in range(1, pairs):
                 difference(k)
         for m in range(moms):
             if 0 <= tick - m < len(stages):
                 stages[tick - m](m)
-        if tick == moms:
+        if tick == moms - 1:
             for k in range(1, pairs):
                 p_far[k].start()
+        if tick == moms:
             difference(0)
+    for k in range(1, pairs):
+        p_core[k].wait_recv()
+        for m in range(moms):
+            dress(m, k)
 
     for copy in p_far + p_core:
         copy.wait_send()
@@ -279,6 +282,20 @@
         copy.wait_send()
     for store in stores.values():
         store.wait()
+
+
+def copy_kernel(src, dst, sem):
+    share = src.shape[0] // PARTS
+    copies = [
+        pltpu.make_async_copy(
+            src.at[pl.ds(n * share, share)], dst.at[pl.ds(n * share, share)], sem.at[n]
+        )
+        for n in range(PARTS)
+    ]
+    for copy in copies:
+        copy.start()
+    for copy in copies:
+        copy.wait()
 
 
 def kernel_shards(eigvecs, perambulator, time_pairs, momenta):
@@ -303,7 +320,7 @@
             [pltpu.VMEM((2, TIMES, 2, 2, 32, vecs), F32) for _ in range(moms)],
             pltpu.VMEM((2, pairs, 2, cols, 2 * vecs), F32),
             pltpu.VMEM((moms * cols * pairs * 8, vecs), F32),
-            pltpu.SemaphoreType.DMA((moms,)),
+            pltpu.SemaphoreType.DMA((moms, pairs)),
             pltpu.SMEM(time_pairs.shape, jnp.int32),
             pltpu.SMEM(momenta.shape, jnp.int32),
             pltpu.VMEM(eig_rows.shape, F32),
@@ -314,14 +331,13 @@
             pltpu.VMEM((depth, 2 * vecs), BF16),
             pltpu.VMEM((sites, 128), F32),
             pltpu.VMEM((moms, 2, 2, 2, 32, vecs), F32),
-            pltpu.VMEM((moms, 2, 2, 32, vecs), F32),
-            pltpu.VMEM((moms, 2, 32, vecs), F32),
+            pltpu.VMEM((moms, 3, 2, 32, vecs), F32),
             pltpu.VMEM((moms, 2, 32, vecs), F32),
             pltpu.VMEM((moms, 2, 32, vecs), F32),
             pltpu.VMEM((pairs, 2, cols, 2 * vecs), F32),
             pltpu.VMEM((pairs, 2, cols, 2 * vecs), F32),
-            pltpu.SemaphoreType.DMA((moms, 8)),
-            pltpu.SemaphoreType.DMA((moms, 8)),
+            pltpu.SemaphoreType.DMA((moms, 9)),
+            pltpu.SemaphoreType.DMA((moms, 9)),
             pltpu.SemaphoreType.DMA((2, pairs)),
             pltpu.SemaphoreType.DMA((2, pairs)),
         ],
@@ -330,6 +346,15 @@
         ),
         name="correlators",
     )(momenta, eig_rows, per_rows, time_pairs)
+    rows = pl.pallas_call(
+        copy_kernel,
+        out_shape=jax.ShapeDtypeStruct(rows.shape, F32),
+        in_specs=[hbm],
+        out_specs=hbm,
+        scratch_shapes=[pltpu.SemaphoreType.DMA((PARTS,))],
+        compiler_params=pltpu.CompilerParams(vmem_limit_bytes=62 * 2**20),
+        name="result",
+    )(rows)
     return (
         rows.reshape(cols, pairs, moms, 4, 2, vecs)
         .transpose(0, 1, 2, 4, 3, 5)

time: 48.1 us -> 109 us (2.27)
  Pallas kernels: 43.5 us -> 109 us
  local copies, waits for them, and re-layouts: 4.41 us -> 0 us
    pallas_call x0 -> x1, Pallas kernels: none -> 64.7 us  [kernel_shards(): pl.pallas_call(copy_kernel, out_shape=jax.ShapeDtypeStruct(rows.shape, F3...]
    unnamed x1 -> x0, local copies, waits for them, and re-layouts: 4.41 us -> none
where the time goes in v2:
time: 109 us
  Pallas kernels  109 us (100%)
    pallas_call x1, Pallas kernels, kernel_shards(): pl.pallas_call(copy_kernel, out_shape=jax.ShapeDtypeStruct(rows.shape, F3...  64.7 us
    pallas_call x1, Pallas kernels, kernel_shards(): pl.pallas_call(functools.partial(correlator_kernel, scale), out_shape=jax...  44.2 us

profile of v2, /device:TPU:1, one launch (start us, length us, event | category | flops | bytes accessed | tf_op | source)
XLA Modules:
  0.0 108.9 jit_solution(7030033522679799519)
XLA Ops:
  0.0 44.2 %correlators.1.src = f32[64,2,4,8,128]{4,3,2,1,0:T(8,128)} custom-call(s32[4,3]{1,0:T(4,128)} %mom_hbm.1, f32[2592,128]{1,0:T(8,128)} %bitcast.11, f32[1024,128]{1,0:T(8,128)} %bitcast.12, s32[2,2]{1,0:T(2,128)} %pairs_hbm.1), custom_call_target="tpu_custom_call" | custom-call | tf_op jit(solution)/shard_map/correlators/pallas_call | solution.py:314
  44.3 64.7 %result.1 = f32[64,2,4,8,128]{4,3,2,1,0:T(8,128)} custom-call(f32[64,2,4,8,128]{4,3,2,1,0:T(8,128)} %correlators.1.src), custom_call_target="tpu_custom_call" | custom-call | tf_op jit(solution)/shard_map/result/pallas_call | solution.py:349

commit v3 on v2

--- a/solution.py
+++ b/solution.py
@@ -47,7 +47,11 @@
     near = slab + 2 - 4 * sub
     cross = near + 1 - 2 * core
     far = (slab + 4) % SLABS
-    tm_peers = (time + 1 - 2 * (time % 2), (time + 2) % TIMES, TIMES - 1 - time)
+    along_x = time + 1 - 2 * (time % 2)
+    along_y = (time + 2) % TIMES
+    first = along_x * (1 - core) + along_y * core
+    second = along_y * (1 - core) + along_x * core
+    tm_peers = (along_x, along_y)
     slab_peers = (sibling, near, cross, far)
 
     loads = [
@@ -119,32 +123,35 @@
     phase[...] = jnp.cos(turns * (2.0 * math.pi / LS))
 
     loads[2].wait()
-    rows = []
+    wide = left.shape[1] // 2
     colours = eig_ref.shape[0] // (2 * sites)
     for c in range(colours):
         real = eig_ref[pl.ds(2 * sites * c, sites, stride=2), :]
         imag = eig_ref[pl.ds(2 * sites * c + 1, sites, stride=2), :]
-        rows.append(jnp.concatenate([real, imag], axis=1))
-    high, low = split(jnp.concatenate(rows, axis=0).T)
-    wide = rows[0].shape[1]
-    left[:wide] = high
-    left[wide:] = low
-
-    def compute(m):
+        high, low = split(jnp.concatenate([real, imag], axis=1).T)
+        left[c, :wide] = high
+        left[c, wide:] = low
+
+    sums = {}
+
+    def compute(m, c):
         cosine = phase[:, m:m + 1]
         sine = phase[:, moms + m:moms + m + 1]
-        for c in range(colours):
-            real = eig_ref[pl.ds(2 * sites * c, sites, stride=2), :]
-            imag = eig_ref[pl.ds(2 * sites * c + 1, sites, stride=2), :]
-            turned = jnp.concatenate(
-                [cosine * real - sine * imag, sine * real + cosine * imag], axis=1
-            )
-            high, low = split(turned)
-            rh[c * sites:(c + 1) * sites, :] = high
-            rl[c * sites:(c + 1) * sites, :] = low
-        coarse = lax.dot_general(left[...], rh[...], NN, preferred_element_type=F32)
-        fine = lax.dot_general(left[:wide], rl[...], NN, preferred_element_type=F32)
+        real = eig_ref[pl.ds(2 * sites * c, sites, stride=2), :]
+        imag = eig_ref[pl.ds(2 * sites * c + 1, sites, stride=2), :]
+        turned = jnp.concatenate(
+            [cosine * real - sine * imag, sine * real + cosine * imag], axis=1
+        )
+        high, low = split(turned)
+        rh[...] = high
+        rl[...] = low
+        coarse = lax.dot_general(left[c], rh[...], NN, preferred_element_type=F32)
+        fine = lax.dot_general(left[c, :wide], rl[...], NN, preferred_element_type=F32)
         got = coarse[:wide] + (coarse[wide:] + fine)
+        sums[m] = got if c == 0 else sums[m] + got
+
+    def spread(m):
+        got = sums.pop(m)
         both = (
             got[:128, :128] + got[128:, 128:],
             got[:128, 128:] - got[128:, :128],
@@ -183,20 +190,26 @@
     def step4(m):
         steps[m, 3].wait_recv()
         done = e_refs[m].at[core, time]
-        for n, peer in enumerate(tm_peers):
+        for n, peer in enumerate((first, second)):
             steps[m, 4, n] = remote(
                 done, done, send_sem.at[m, 5 + n], recv_sem.at[m, 5 + n], "tm", peer
             )
             steps[m, 4, n].start()
 
     def step5(m):
-        for n in range(len(tm_peers)):
-            steps[m, 4, n].wait_recv()
+        steps[m, 4, 0].wait_recv()
+        done = e_refs[m].at[core, first]
+        steps[m, 4, 2] = remote(done, done, send_sem.at[m, 7], recv_sem.at[m, 7], "tm", second)
+        steps[m, 4, 2].start()
+
+    def step6(m):
+        steps[m, 4, 1].wait_recv()
+        steps[m, 4, 2].wait_recv()
         done = e_refs[m].at[core]
         steps[m, 5] = remote(done, done, send_sem.at[m, 8], recv_sem.at[m, 8], "slab", sibling)
         steps[m, 5].start()
 
-    def step6(m):
+    def step7(m):
         steps[m, 5].wait_recv()
         if m == 0:
             p_core[0].wait_recv()
@@ -255,26 +268,36 @@
         stores[m, k].start()
 
     stores = {}
-    stages = (step1, step2, step3, step4, step5, step6)
-    ticks = moms + len(stages) - 1
-    for tick in range(ticks):
-        if tick < moms:
-            compute(tick)
-        if tick == ticks - 1:
+    stages = (step1, step2, step3, step4, step5, step6, step7)
+    offsets = (0, 1, 3, 4, 6, 7, 9)
+    plan = {}
+    for m in range(moms):
+        ready = colours * (m + 1) - 1
+        for stage, offset in zip(stages, offsets):
+            plan.setdefault(ready + offset, []).append((stage, m))
+    last = max(plan)
+    for tick in range(last):
+        if tick < colours * moms:
+            compute(tick // colours, tick % colours)
+            if tick % colours == colours - 1:
+                spread(tick // colours)
+        for stage, m in plan.get(tick, ()):
+            stage(m)
+        if tick == colours * (moms - 1):
+            difference(0)
+        if tick == colours * (moms - 1) - 1:
+            for k in range(1, pairs):
+                p_far[k].start()
+        if tick == last - 2:
             for k in range(1, pairs):
                 difference(k)
-        for m in range(moms):
-            if 0 <= tick - m < len(stages):
-                stages[tick - m](m)
-        if tick == moms - 1:
-            for k in range(1, pairs):
-                p_far[k].start()
-        if tick == moms:
-            difference(0)
     for k in range(1, pairs):
         p_core[k].wait_recv()
-        for m in range(moms):
+        for m in range(moms - 1):
             dress(m, k)
+    step7(moms - 1)
+    for k in range(1, pairs):
+        dress(moms - 1, k)
 
     for copy in p_far + p_core:
         copy.wait_send()
@@ -284,18 +307,20 @@
         store.wait()
 
 
-def copy_kernel(src, dst, sem):
+def copy_kernel(src, dst, held, in_sem, out_sem):
     share = src.shape[0] // PARTS
-    copies = [
-        pltpu.make_async_copy(
-            src.at[pl.ds(n * share, share)], dst.at[pl.ds(n * share, share)], sem.at[n]
-        )
-        for n in range(PARTS)
-    ]
-    for copy in copies:
-        copy.start()
-    for copy in copies:
-        copy.wait()
+    loads, stores = [], []
+    for n in range(PARTS):
+        part = pl.ds(n * share, share)
+        loads.append(pltpu.make_async_copy(src.at[part], held.at[part], in_sem.at[n]))
+        stores.append(pltpu.make_async_copy(held.at[part], dst.at[part], out_sem.at[n]))
+    for load in loads:
+        load.start()
+    for load, store in zip(loads, stores):
+        load.wait()
+        store.start()
+    for store in stores:
+        store.wait()
 
 
 def kernel_shards(eigvecs, perambulator, time_pairs, momenta):
@@ -310,7 +335,6 @@
         .reshape(cols * pairs * 8, vecs)
     )
     hbm = pl.BlockSpec(memory_space=pltpu.HBM)
-    depth = colours * sites
     rows = pl.pallas_call(
         functools.partial(correlator_kernel, scale),
         out_shape=jax.ShapeDtypeStruct((cols, pairs, moms, 8, vecs), F32),
@@ -326,9 +350,9 @@
             pltpu.VMEM(eig_rows.shape, F32),
             pltpu.VMEM(per_rows.shape, F32),
             pltpu.SemaphoreType.DMA((4,)),
-            pltpu.VMEM((4 * vecs, depth), BF16),
-            pltpu.VMEM((depth, 2 * vecs), BF16),
-            pltpu.VMEM((depth, 2 * vecs), BF16),
+            pltpu.VMEM((colours, 4 * vecs, sites), BF16),
+            pltpu.VMEM((sites, 2 * vecs), BF16),
+            pltpu.VMEM((sites, 2 * vecs), BF16),
             pltpu.VMEM((sites, 128), F32),
             pltpu.VMEM((moms, 2, 2, 2, 32, vecs), F32),
             pltpu.VMEM((moms, 3, 2, 32, vecs), F32),
@@ -351,7 +375,11 @@
         out_shape=jax.ShapeDtypeStruct(rows.shape, F32),
         in_specs=[hbm],
         out_specs=hbm,
-        scratch_shapes=[pltpu.SemaphoreType.DMA((PARTS,))],
+        scratch_shapes=[
+            pltpu.VMEM(rows.shape, F32),
+            pltpu.SemaphoreType.DMA((PARTS,)),
+            pltpu.SemaphoreType.DMA((PARTS,)),
+        ],
         compiler_params=pltpu.CompilerParams(vmem_limit_bytes=62 * 2**20),
         name="result",
     )(rows)

time: 109 us -> 56 us (0.51)
  Pallas kernels: 109 us -> 55.9 us
    pallas_call x1, Pallas kernels: 64.7 us -> 2.42 us  [kernel_shards(): pl.pallas_call(copy_kernel, out_shape=jax.ShapeDtypeStruct(rows.shape, F3...]
    pallas_call x1, Pallas kernels: 44.2 us -> 53.5 us  [kernel_shards(): pl.pallas_call(functools.partial(correlator_kernel, scale), out_shape=jax...]
where the time goes in v3:
time: 56 us; the launch traced here: 55.9 us
  Pallas kernels  55.9 us (100%)
    pallas_call x1, Pallas kernels, kernel_shards(): pl.pallas_call(functools.partial(correlator_kernel, scale), out_shape=jax...  53.5 us
    pallas_call x1, Pallas kernels, kernel_shards(): pl.pallas_call(copy_kernel, out_shape=jax.ShapeDtypeStruct(rows.shape, F3...  2.42 us

profile of v3, /device:TPU:1, one launch (start us, length us, event | category | flops | bytes accessed | tf_op | source)
XLA Modules:
  0.0 55.9 jit_solution(4360023172194494479)
XLA Ops:
  0.0 53.5 %correlators.1.src = f32[64,2,4,8,128]{4,3,2,1,0:T(8,128)} custom-call(s32[4,3]{1,0:T(4,128)} %mom_hbm.1, f32[2592,128]{1,0:T(8,128)} %bitcast.11, f32[1024,128]{1,0:T(8,128)} %bitcast.12, s32[2,2]{1,0:T(2,128)} %pairs_hbm.1), custom_call_target="tpu_custom_call" | custom-call | tf_op jit(solution)/shard_map/correlators/pallas_call | solution.py:338
  53.5 2.4 %result.1 = f32[64,2,4,8,128]{4,3,2,1,0:T(8,128)} custom-call(f32[64,2,4,8,128]{4,3,2,1,0:T(8,128)} %correlators.1.src), custom_call_target="tpu_custom_call" | custom-call | tf_op jit(solution)/shard_map/result/pallas_call | solution.py:373

commit v4 on v2

--- a/solution.py
+++ b/solution.py
@@ -47,7 +47,11 @@
     near = slab + 2 - 4 * sub
     cross = near + 1 - 2 * core
     far = (slab + 4) % SLABS
-    tm_peers = (time + 1 - 2 * (time % 2), (time + 2) % TIMES, TIMES - 1 - time)
+    along_x = time + 1 - 2 * (time % 2)
+    along_y = (time + 2) % TIMES
+    first = along_x * (1 - core) + along_y * core
+    second = along_y * (1 - core) + along_x * core
+    tm_peers = (along_x, along_y)
     slab_peers = (sibling, near, cross, far)
 
     loads = [
@@ -120,13 +124,13 @@
 
     loads[2].wait()
     rows = []
+    wide = left.shape[0] // 2
     colours = eig_ref.shape[0] // (2 * sites)
     for c in range(colours):
         real = eig_ref[pl.ds(2 * sites * c, sites, stride=2), :]
         imag = eig_ref[pl.ds(2 * sites * c + 1, sites, stride=2), :]
         rows.append(jnp.concatenate([real, imag], axis=1))
     high, low = split(jnp.concatenate(rows, axis=0).T)
-    wide = rows[0].shape[1]
     left[:wide] = high
     left[wide:] = low
 
@@ -183,25 +187,27 @@
     def step4(m):
         steps[m, 3].wait_recv()
         done = e_refs[m].at[core, time]
-        for n, peer in enumerate(tm_peers):
+        for n, peer in enumerate((first, second)):
             steps[m, 4, n] = remote(
                 done, done, send_sem.at[m, 5 + n], recv_sem.at[m, 5 + n], "tm", peer
             )
             steps[m, 4, n].start()
 
     def step5(m):
-        for n in range(len(tm_peers)):
-            steps[m, 4, n].wait_recv()
+        steps[m, 4, 0].wait_recv()
+        done = e_refs[m].at[core, first]
+        steps[m, 4, 2] = remote(done, done, send_sem.at[m, 7], recv_sem.at[m, 7], "tm", second)
+        steps[m, 4, 2].start()
+
+    def step6(m):
+        steps[m, 4, 1].wait_recv()
+        steps[m, 4, 2].wait_recv()
         done = e_refs[m].at[core]
         steps[m, 5] = remote(done, done, send_sem.at[m, 8], recv_sem.at[m, 8], "slab", sibling)
         steps[m, 5].start()
 
-    def step6(m):
+    def step7(m):
         steps[m, 5].wait_recv()
-        if m == 0:
-            p_core[0].wait_recv()
-            loads[3].wait()
-        dress(m, 0)
 
     rows_each = cols * 8
 
@@ -255,26 +261,37 @@
         stores[m, k].start()
 
     stores = {}
-    stages = (step1, step2, step3, step4, step5, step6)
+    stages = (step1, step2, step3, step4, step5, step6, step7)
+    loads[3].wait()
     ticks = moms + len(stages) - 1
-    for tick in range(ticks):
+    for tick in range(ticks - 1):
         if tick < moms:
             compute(tick)
-        if tick == ticks - 1:
+        if tick == moms - 2:
             for k in range(1, pairs):
-                difference(k)
+                p_far[k].start()
+        arrived = None
         for m in range(moms):
             if 0 <= tick - m < len(stages):
                 stages[tick - m](m)
-        if tick == moms - 1:
+                if stages[tick - m] is step7:
+                    arrived = m
+        if tick == moms + 1:
+            difference(0)
+        if tick == ticks - 2:
             for k in range(1, pairs):
-                p_far[k].start()
-        if tick == moms:
-            difference(0)
+                difference(k)
+        if arrived is not None:
+            if arrived == 0:
+                p_core[0].wait_recv()
+            dress(arrived, 0)
     for k in range(1, pairs):
         p_core[k].wait_recv()
-        for m in range(moms):
+        for m in range(moms - 1):
             dress(m, k)
+    step7(moms - 1)
+    for k in range(pairs):
+        dress(moms - 1, k)
 
     for copy in p_far + p_core:
         copy.wait_send()
@@ -284,18 +301,20 @@
         store.wait()
 
 
-def copy_kernel(src, dst, sem):
+def copy_kernel(src, dst, held, in_sem, out_sem):
     share = src.shape[0] // PARTS
-    copies = [
-        pltpu.make_async_copy(
-            src.at[pl.ds(n * share, share)], dst.at[pl.ds(n * share, share)], sem.at[n]
-        )
-        for n in range(PARTS)
-    ]
-    for copy in copies:
-        copy.start()
-    for copy in copies:
-        copy.wait()
+    loads, stores = [], []
+    for n in range(PARTS):
+        part = pl.ds(n * share, share)
+        loads.append(pltpu.make_async_copy(src.at[part], held.at[part], in_sem.at[n]))
+        stores.append(pltpu.make_async_copy(held.at[part], dst.at[part], out_sem.at[n]))
+    for load in loads:
+        load.start()
+    for load, store in zip(loads, stores):
+        load.wait()
+        store.start()
+    for store in stores:
+        store.wait()
 
 
 def kernel_shards(eigvecs, perambulator, time_pairs, momenta):
@@ -309,8 +328,8 @@
         .transpose(0, 1, 3, 2, 4)
         .reshape(cols * pairs * 8, vecs)
     )
+    depth = colours * sites
     hbm = pl.BlockSpec(memory_space=pltpu.HBM)
-    depth = colours * sites
     rows = pl.pallas_call(
         functools.partial(correlator_kernel, scale),
         out_shape=jax.ShapeDtypeStruct((cols, pairs, moms, 8, vecs), F32),
@@ -351,7 +370,11 @@
         out_shape=jax.ShapeDtypeStruct(rows.shape, F32),
         in_specs=[hbm],
         out_specs=hbm,
-        scratch_shapes=[pltpu.SemaphoreType.DMA((PARTS,))],
+        scratch_shapes=[
+            pltpu.VMEM(rows.shape, F32),
+            pltpu.SemaphoreType.DMA((PARTS,)),
+            pltpu.SemaphoreType.DMA((PARTS,)),
+        ],
         compiler_params=pltpu.CompilerParams(vmem_limit_bytes=62 * 2**20),
         name="result",
     )(rows)

time: 109 us -> 49.6 us (0.46)
  Pallas kernels: 109 us -> 49.5 us
    pallas_call x1, Pallas kernels: 64.7 us -> 2.42 us  [kernel_shards(): pl.pallas_call(copy_kernel, out_shape=jax.ShapeDtypeStruct(rows.shape, F3...]
    pallas_call x1, Pallas kernels: 44.2 us -> 47 us  [kernel_shards(): pl.pallas_call(functools.partial(correlator_kernel, scale), out_shape=jax...]
where the time goes in v4:
time: 49.6 us; the launch traced here: 49.5 us
  Pallas kernels  49.5 us (100%)
    pallas_call x1, Pallas kernels, kernel_shards(): pl.pallas_call(functools.partial(correlator_kernel, scale), out_shape=jax...  47 us
    pallas_call x1, Pallas kernels, kernel_shards(): pl.pallas_call(copy_kernel, out_shape=jax.ShapeDtypeStruct(rows.shape, F3...  2.42 us

profile of v4, /device:TPU:1, one launch (start us, length us, event | category | flops | bytes accessed | tf_op | source)
XLA Modules:
  0.0 49.5 jit_solution(16283701603226974475)
XLA Ops:
  0.0 47.0 %correlators.1.src = f32[64,2,4,8,128]{4,3,2,1,0:T(8,128)} custom-call(s32[4,3]{1,0:T(4,128)} %mom_hbm.1, f32[2592,128]{1,0:T(8,128)} %bitcast.11, f32[1024,128]{1,0:T(8,128)} %bitcast.12, s32[2,2]{1,0:T(2,128)} %pairs_hbm.1), custom_call_target="tpu_custom_call" | custom-call | tf_op jit(solution)/shard_map/correlators/pallas_call | solution.py:333
  47.1 2.4 %result.1 = f32[64,2,4,8,128]{4,3,2,1,0:T(8,128)} custom-call(f32[64,2,4,8,128]{4,3,2,1,0:T(8,128)} %correlators.1.src), custom_call_target="tpu_custom_call" | custom-call | tf_op jit(solution)/shard_map/result/pallas_call | solution.py:368

commit v5 on v4

--- a/solution.py
+++ b/solution.py
@@ -35,8 +35,8 @@
 
 
 def correlator_kernel(
-    scale, mom_hbm, eig_hbm, per_hbm, pairs_hbm, out_hbm,
-    e_refs, d_ref, out_ref, out_sem, pairs_ref, mom_ref, eig_ref, per_ref, load_sem, left, rh, rl, phase, part, r1, h2, r3, psend, precv,
+    scale, sites, mom_hbm, eig_hbm, per_hbm, pairs_hbm, out_hbm,
+    e_refs, d_ref, out_ref, out_sem, pairs_ref, mom_ref, eig_ref, per_ref, load_sem, left, rh, rl, flat, phase, part, r1, h2, r3, psend, precv,
     send_sem, recv_sem, psend_sem, precv_sem,
 ):
     slab = lax.axis_index("slab")
@@ -47,11 +47,7 @@
     near = slab + 2 - 4 * sub
     cross = near + 1 - 2 * core
     far = (slab + 4) % SLABS
-    along_x = time + 1 - 2 * (time % 2)
-    along_y = (time + 2) % TIMES
-    first = along_x * (1 - core) + along_y * core
-    second = along_y * (1 - core) + along_x * core
-    tm_peers = (along_x, along_y)
+    tm_peers = (time + 1 - 2 * (time % 2), (time + 2) % TIMES, TIMES - 1 - time)
     slab_peers = (sibling, near, cross, far)
 
     loads = [
@@ -106,52 +102,61 @@
     loads[1].wait()
 
     moms = mom_ref.shape[0]
-    sites = phase.shape[0]
-    site = (lax.broadcasted_iota(jnp.int32, (sites, 128), 0) + slab * sites).astype(F32)
-    lane = lax.broadcasted_iota(jnp.int32, (sites, 128), 1)
+    colours = eig_ref.shape[0] // (2 * sites)
+    depth = colours * sites
+    place = lax.broadcasted_iota(jnp.int32, (2 * moms, depth), 1).astype(F32)
+    kind = lax.broadcasted_iota(jnp.int32, (2 * moms, depth), 0)
+    site = place - sites * floor_div(place, sites) + (slab * sites).astype(F32)
     row = floor_div(site, LS)
     plane = floor_div(row, LS)
     coords = (site - LS * row, row - LS * plane, plane)
-    turns = jnp.zeros((sites, 128), F32)
+    turns = jnp.zeros((2 * moms, depth), F32)
     for m in range(moms):
         mine = mom_ref[m, 0].astype(F32) * coords[0]
         mine = mine + mom_ref[m, 1].astype(F32) * coords[1]
         mine = mine + mom_ref[m, 2].astype(F32) * coords[2]
-        turns = jnp.where(lane % moms == m, mine, turns)
+        turns = jnp.where(kind % moms == m, mine, turns)
     turns = turns - LS * floor_div(turns, LS)
-    turns = jnp.where(lane >= moms, turns - LS / 4, turns)
+    turns = jnp.where(kind >= moms, turns - LS / 4, turns)
     phase[...] = jnp.cos(turns * (2.0 * math.pi / LS))
 
     loads[2].wait()
+    vecs = eig_ref.shape[1]
+    wide = 2 * vecs
     rows = []
-    wide = left.shape[0] // 2
-    colours = eig_ref.shape[0] // (2 * sites)
     for c in range(colours):
         real = eig_ref[pl.ds(2 * sites * c, sites, stride=2), :]
         imag = eig_ref[pl.ds(2 * sites * c + 1, sites, stride=2), :]
         rows.append(jnp.concatenate([real, imag], axis=1))
-    high, low = split(jnp.concatenate(rows, axis=0).T)
-    left[:wide] = high
-    left[wide:] = low
+    whole = jnp.concatenate(rows, axis=0)
+    high, low = split(whole)
+    rh[...] = high
+    rl[...] = low
+    flat[...] = whole.T
+
+    def turn(m):
+        cosine = phase[m:m + 1, :]
+        sine = phase[moms + m:moms + m + 1, :]
+        real = flat[:vecs, :]
+        imag = flat[vecs:, :]
+        slot = m % 2
+        for n, value in enumerate(
+            (cosine * real - sine * imag, sine * real + cosine * imag)
+        ):
+            high, low = split(value)
+            left[slot, n * vecs:(n + 1) * vecs] = high
+            left[slot, wide + n * vecs:wide + (n + 1) * vecs] = low
 
     def compute(m):
-        cosine = phase[:, m:m + 1]
-        sine = phase[:, moms + m:moms + m + 1]
-        for c in range(colours):
-            real = eig_ref[pl.ds(2 * sites * c, sites, stride=2), :]
-            imag = eig_ref[pl.ds(2 * sites * c + 1, sites, stride=2), :]
-            turned = jnp.concatenate(
-                [cosine * real - sine * imag, sine * real + cosine * imag], axis=1
-            )
-            high, low = split(turned)
-            rh[c * sites:(c + 1) * sites, :] = high
-            rl[c * sites:(c + 1) * sites, :] = low
-        coarse = lax.dot_general(left[...], rh[...], NN, preferred_element_type=F32)
-        fine = lax.dot_general(left[:wide], rl[...], NN, preferred_element_type=F32)
+        slot = m % 2
+        coarse = lax.dot_general(left[slot], rh[...], NN, preferred_element_type=F32)
+        fine = lax.dot_general(left[slot, :wide], rl[...], NN, preferred_element_type=F32)
+        if m + 1 < moms:
+            turn(m + 1)
         got = coarse[:wide] + (coarse[wide:] + fine)
         both = (
-            got[:128, :128] + got[128:, 128:],
-            got[:128, 128:] - got[128:, :128],
+            (got[:vecs, :vecs] + got[vecs:, vecs:]).T,
+            (got[vecs:, :vecs] - got[:vecs, vecs:]).T,
         )
         for half in range(2):
             for u in range(2):
@@ -187,26 +192,20 @@
     def step4(m):
         steps[m, 3].wait_recv()
         done = e_refs[m].at[core, time]
-        for n, peer in enumerate((first, second)):
+        for n, peer in enumerate(tm_peers):
             steps[m, 4, n] = remote(
                 done, done, send_sem.at[m, 5 + n], recv_sem.at[m, 5 + n], "tm", peer
             )
             steps[m, 4, n].start()
 
     def step5(m):
-        steps[m, 4, 0].wait_recv()
-        done = e_refs[m].at[core, first]
-        steps[m, 4, 2] = remote(done, done, send_sem.at[m, 7], recv_sem.at[m, 7], "tm", second)
-        steps[m, 4, 2].start()
-
-    def step6(m):
-        steps[m, 4, 1].wait_recv()
-        steps[m, 4, 2].wait_recv()
+        for n in range(len(tm_peers)):
+            steps[m, 4, n].wait_recv()
         done = e_refs[m].at[core]
         steps[m, 5] = remote(done, done, send_sem.at[m, 8], recv_sem.at[m, 8], "slab", sibling)
         steps[m, 5].start()
 
-    def step7(m):
+    def step6(m):
         steps[m, 5].wait_recv()
 
     rows_each = cols * 8
@@ -261,22 +260,23 @@
         stores[m, k].start()
 
     stores = {}
-    stages = (step1, step2, step3, step4, step5, step6, step7)
+    stages = (step1, step2, step3, step4, step5, step6)
     loads[3].wait()
+    turn(0)
     ticks = moms + len(stages) - 1
     for tick in range(ticks - 1):
         if tick < moms:
             compute(tick)
-        if tick == moms - 2:
-            for k in range(1, pairs):
-                p_far[k].start()
         arrived = None
         for m in range(moms):
             if 0 <= tick - m < len(stages):
                 stages[tick - m](m)
-                if stages[tick - m] is step7:
+                if stages[tick - m] is step6:
                     arrived = m
-        if tick == moms + 1:
+        if tick == moms - 1:
+            for k in range(1, pairs):
+                p_far[k].start()
+        if tick == moms:
             difference(0)
         if tick == ticks - 2:
             for k in range(1, pairs):
@@ -289,7 +289,7 @@
         p_core[k].wait_recv()
         for m in range(moms - 1):
             dress(m, k)
-    step7(moms - 1)
+    step6(moms - 1)
     for k in range(pairs):
         dress(moms - 1, k)
 
@@ -331,7 +331,7 @@
     depth = colours * sites
     hbm = pl.BlockSpec(memory_space=pltpu.HBM)
     rows = pl.pallas_call(
-        functools.partial(correlator_kernel, scale),
+        functools.partial(correlator_kernel, scale, sites),
         out_shape=jax.ShapeDtypeStruct((cols, pairs, moms, 8, vecs), F32),
         in_specs=[hbm, hbm, hbm, hbm],
         out_specs=hbm,
@@ -345,10 +345,11 @@
             pltpu.VMEM(eig_rows.shape, F32),
             pltpu.VMEM(per_rows.shape, F32),
             pltpu.SemaphoreType.DMA((4,)),
-            pltpu.VMEM((4 * vecs, depth), BF16),
+            pltpu.VMEM((2, 4 * vecs, depth), BF16),
             pltpu.VMEM((depth, 2 * vecs), BF16),
             pltpu.VMEM((depth, 2 * vecs), BF16),
-            pltpu.VMEM((sites, 128), F32),
+            pltpu.VMEM((2 * vecs, depth), F32),
+            pltpu.VMEM((2 * moms, depth), F32),
             pltpu.VMEM((moms, 2, 2, 2, 32, vecs), F32),
             pltpu.VMEM((moms, 3, 2, 32, vecs), F32),
             pltpu.VMEM((moms, 2, 32, vecs), F32),

time: 49.6 us -> 47 us (0.948)
  Pallas kernels: 49.5 us -> 46.8 us
    pallas_call x1, Pallas kernels: 47 us -> 44.4 us  [kernel_shards(): pl.pallas_call(functools.partial(correlator_kernel, scale, sites), out_sh...]
where the time goes in v5:
time: 47 us; the launch traced here: 46.8 us
  Pallas kernels  46.8 us (100%)
    pallas_call x1, Pallas kernels, kernel_shards(): pl.pallas_call(functools.partial(correlator_kernel, scale, sites), out_sh...  44.4 us
    pallas_call x1, Pallas kernels, kernel_shards(): pl.pallas_call(copy_kernel, out_shape=jax.ShapeDtypeStruct(rows.shape, F3...  2.42 us

profile of v5, /device:TPU:1, one launch (start us, length us, event | category | flops | bytes accessed | tf_op | source)
XLA Modules:
  0.0 46.8 jit_solution(9528264934138114803)
XLA Ops:
  0.0 44.4 %correlators.1.src = f32[64,2,4,8,128]{4,3,2,1,0:T(8,128)} custom-call(s32[4,3]{1,0:T(4,128)} %mom_hbm.1, f32[2592,128]{1,0:T(8,128)} %bitcast.11, f32[1024,128]{1,0:T(8,128)} %bitcast.12, s32[2,2]{1,0:T(2,128)} %pairs_hbm.1), custom_call_target="tpu_custom_call" | custom-call | tf_op jit(solution)/shard_map/correlators/pallas_call | solution.py:333
  44.4 2.4 %result.1 = f32[64,2,4,8,128]{4,3,2,1,0:T(8,128)} custom-call(f32[64,2,4,8,128]{4,3,2,1,0:T(8,128)} %correlators.1.src), custom_call_target="tpu_custom_call" | custom-call | tf_op jit(solution)/shard_map/result/pallas_call | solution.py:369

commit v6 on v5

--- a/solution.py
+++ b/solution.py
@@ -84,21 +84,43 @@
             device_id={axis: peer}, device_id_type=pl.DeviceIdType.MESH,
         )
 
+    pieces = [(p, pl.ds(16 * j, 16)) for p in range(2) for j in range(cols // 16)]
+
+    def start(copies):
+        for copy in copies:
+            copy.start()
+
+    def wait_recv(copies):
+        for copy in copies:
+            copy.wait_recv()
+
     p_far = [
-        remote(psend.at[k], precv.at[k], psend_sem.at[0, k], precv_sem.at[0, k], "slab", far)
+        [
+            remote(
+                psend.at[k, p, part_rows], precv.at[k, p, part_rows],
+                psend_sem.at[0, k, n], precv_sem.at[0, k, n], "slab", far,
+            )
+            for n, (p, part_rows) in enumerate(pieces)
+        ]
         for k in range(pairs)
     ]
     p_core = [
-        remote(d_ref.at[core, k], d_ref.at[core, k], psend_sem.at[1, k], precv_sem.at[1, k], "slab", sibling)
+        [
+            remote(
+                d_ref.at[core, k, p], d_ref.at[core, k, p],
+                psend_sem.at[1, k, p], precv_sem.at[1, k, p], "slab", sibling,
+            )
+            for p in range(2)
+        ]
         for k in range(pairs)
     ]
 
     def difference(k):
-        p_far[k].wait_recv()
+        wait_recv(p_far[k])
         d_ref[core, k] = psend[k] - precv[k]
-        p_core[k].start()
-
-    p_far[0].start()
+        start(p_core[k])
+
+    start(p_far[0])
     loads[1].wait()
 
     moms = mom_ref.shape[0]
@@ -191,22 +213,29 @@
 
     def step4(m):
         steps[m, 3].wait_recv()
-        done = e_refs[m].at[core, time]
-        for n, peer in enumerate(tm_peers):
-            steps[m, 4, n] = remote(
-                done, done, send_sem.at[m, 5 + n], recv_sem.at[m, 5 + n], "tm", peer
+        for u in range(2):
+            done = e_refs[m].at[core, time, u]
+            for n, peer in enumerate(tm_peers):
+                spot = 5 + 3 * u + n
+                steps[m, 4, u, n] = remote(
+                    done, done, send_sem.at[m, spot], recv_sem.at[m, spot], "tm", peer
+                )
+                steps[m, 4, u, n].start()
+
+    def step5(m):
+        for u in range(2):
+            for n in range(len(tm_peers)):
+                steps[m, 4, u, n].wait_recv()
+        for t in range(TIMES):
+            done = e_refs[m].at[core, t]
+            steps[m, 5, t] = remote(
+                done, done, send_sem.at[m, 11 + t], recv_sem.at[m, 11 + t], "slab", sibling
             )
-            steps[m, 4, n].start()
-
-    def step5(m):
-        for n in range(len(tm_peers)):
-            steps[m, 4, n].wait_recv()
-        done = e_refs[m].at[core]
-        steps[m, 5] = remote(done, done, send_sem.at[m, 8], recv_sem.at[m, 8], "slab", sibling)
-        steps[m, 5].start()
+            steps[m, 5, t].start()
 
     def step6(m):
-        steps[m, 5].wait_recv()
+        for t in range(TIMES):
+            steps[m, 5, t].wait_recv()
 
     rows_each = cols * 8
 
@@ -275,7 +304,7 @@
                     arrived = m
         if tick == moms - 1:
             for k in range(1, pairs):
-                p_far[k].start()
+                start(p_far[k])
         if tick == moms:
             difference(0)
         if tick == ticks - 2:
@@ -283,18 +312,19 @@
                 difference(k)
         if arrived is not None:
             if arrived == 0:
-                p_core[0].wait_recv()
+                wait_recv(p_core[0])
             dress(arrived, 0)
     for k in range(1, pairs):
-        p_core[k].wait_recv()
+        wait_recv(p_core[k])
         for m in range(moms - 1):
             dress(m, k)
     step6(moms - 1)
     for k in range(pairs):
         dress(moms - 1, k)
 
-    for copy in p_far + p_core:
-        copy.wait_send()
+    for copies in p_far + p_core:
+        for copy in copies:
+            copy.wait_send()
     for copy in steps.values():
         copy.wait_send()
     for store in stores.values():
@@ -356,10 +386,10 @@
             pltpu.VMEM((moms, 2, 32, vecs), F32),
             pltpu.VMEM((pairs, 2, cols, 2 * vecs), F32),
             pltpu.VMEM((pairs, 2, cols, 2 * vecs), F32),
-            pltpu.SemaphoreType.DMA((moms, 9)),
-            pltpu.SemaphoreType.DMA((moms, 9)),
-            pltpu.SemaphoreType.DMA((2, pairs)),
-            pltpu.SemaphoreType.DMA((2, pairs)),
+            pltpu.SemaphoreType.DMA((moms, 15)),
+            pltpu.SemaphoreType.DMA((moms, 15)),
+            pltpu.SemaphoreType.DMA((2, pairs, cols // 8)),
+            pltpu.SemaphoreType.DMA((2, pairs, cols // 8)),
         ],
         compiler_params=pltpu.CompilerParams(
             collective_id=0, has_side_effects=True, vmem_limit_bytes=61 * 2**20

time: 47 us -> 48 us (1.021)
  Pallas kernels: 46.8 us -> 47.8 us
    pallas_call x1, Pallas kernels: 44.4 us -> 45.4 us  [kernel_shards(): pl.pallas_call(functools.partial(correlator_kernel, scale, sites), out_sh...]
where the time goes in v6:
time: 48 us; the launch traced here: 47.8 us
  Pallas kernels  47.8 us (100%)
    pallas_call x1, Pallas kernels, kernel_shards(): pl.pallas_call(functools.partial(correlator_kernel, scale, sites), out_sh...  45.4 us
    pallas_call x1, Pallas kernels, kernel_shards(): pl.pallas_call(copy_kernel, out_shape=jax.ShapeDtypeStruct(rows.shape, F3...  2.42 us

profile of v6, /device:TPU:1, one launch (start us, length us, event | category | flops | bytes accessed | tf_op | source)
XLA Modules:
  0.0 47.8 jit_solution(12535026013700487440)
XLA Ops:
  0.0 45.4 %correlators.1.src = f32[64,2,4,8,128]{4,3,2,1,0:T(8,128)} custom-call(s32[4,3]{1,0:T(4,128)} %mom_hbm.1, f32[2592,128]{1,0:T(8,128)} %bitcast.11, f32[1024,128]{1,0:T(8,128)} %bitcast.12, s32[2,2]{1,0:T(2,128)} %pairs_hbm.1), custom_call_target="tpu_custom_call" | custom-call | tf_op jit(solution)/shard_map/correlators/pallas_call | solution.py:363
  45.4 2.4 %result.1 = f32[64,2,4,8,128]{4,3,2,1,0:T(8,128)} custom-call(f32[64,2,4,8,128]{4,3,2,1,0:T(8,128)} %correlators.1.src), custom_call_target="tpu_custom_call" | custom-call | tf_op jit(solution)/shard_map/result/pallas_call | solution.py:399

commit v7 on v5

--- a/solution.py
+++ b/solution.py
@@ -267,18 +267,18 @@
     for tick in range(ticks - 1):
         if tick < moms:
             compute(tick)
+        if tick == moms - 1:
+            for k in range(1, pairs):
+                p_far[k].start()
         arrived = None
         for m in range(moms):
             if 0 <= tick - m < len(stages):
                 stages[tick - m](m)
                 if stages[tick - m] is step6:
                     arrived = m
-        if tick == moms - 1:
-            for k in range(1, pairs):
-                p_far[k].start()
         if tick == moms:
             difference(0)
-        if tick == ticks - 2:
+        if tick == ticks - 3:
             for k in range(1, pairs):
                 difference(k)
         if arrived is not None:

time: 47 us -> 47.7 us (1.015); the launches traced: 46.8 us -> 46.9 us
  no operation moved by 1% of the time
where the time goes in v7:
time: 47.7 us; the launch traced here: 46.9 us
  Pallas kernels  46.9 us (98%)
    pallas_call x1, Pallas kernels, kernel_shards(): pl.pallas_call(functools.partial(correlator_kernel, scale, sites), out_sh...  44.5 us
    pallas_call x1, Pallas kernels, kernel_shards(): pl.pallas_call(copy_kernel, out_shape=jax.ShapeDtypeStruct(rows.shape, F3...  2.42 us

profile of v7, /device:TPU:1, one launch (start us, length us, event | category | flops | bytes accessed | tf_op | source)
XLA Modules:
  0.0 46.9 jit_solution(6979867003950430280)
XLA Ops:
  0.0 44.5 %correlators.1.src = f32[64,2,4,8,128]{4,3,2,1,0:T(8,128)} custom-call(s32[4,3]{1,0:T(4,128)} %mom_hbm.1, f32[2592,128]{1,0:T(8,128)} %bitcast.11, f32[1024,128]{1,0:T(8,128)} %bitcast.12, s32[2,2]{1,0:T(2,128)} %pairs_hbm.1), custom_call_target="tpu_custom_call" | custom-call | tf_op jit(solution)/shard_map/correlators/pallas_call | solution.py:333
  44.5 2.4 %result.1 = f32[64,2,4,8,128]{4,3,2,1,0:T(8,128)} custom-call(f32[64,2,4,8,128]{4,3,2,1,0:T(8,128)} %correlators.1.src), custom_call_target="tpu_custom_call" | custom-call | tf_op jit(solution)/shard_map/result/pallas_call | solution.py:369
